TPU v7x, 32 devices: a whole 2x2x4 slice. The times are simulated.
32 devices in a mesh: groups: 2 (over y), tensor: 8 (over z, x), dp: 2 (over core).
Axes of the slice: x: 2, y: 2, z: 4, core: 2. Of those that a mesh axis runs over, the one named last changes fastest.
Arguments:
- tokens: bfloat16 [512, 8192], P(('groups', 'dp'), 'tensor'), parts along dimension 0, may hold values from -6 to 6
- gate_weight: bfloat16 [8192, 16384], P('dp', 'tensor'), may hold values from -0.09375 to 0.09375
- up_weight: bfloat16 [8192, 16384], P('dp', 'tensor'), may hold values from -0.09375 to 0.09375
- gate_mask: int32 [128, 256], P('dp', 'tensor'), may hold values from 0 to 1, as said below
- up_mask: int32 [128, 256], P('dp', 'tensor'), may hold values from 0 to 1, as said below
- cotangent: bfloat16 [512, 16384], P(('groups', 'dp'), 'tensor'), parts along dimension 0, may hold values from -6 to 6
Outputs:
- hidden: bfloat16 [512, 16384], P(('groups', 'dp'), 'tensor'), parts along dimension 0
- grad_input: bfloat16 [512, 8192], P(('groups', 'dp'), 'tensor'), parts along dimension 0
- grad_gate: bfloat16 [8192, 32768], P('dp', ('groups', 'tensor')), parts along dimension 1
- grad_up: bfloat16 [8192, 32768], P('dp', ('groups', 'tensor')), parts along dimension 1
There are 2 independent parts, one for each index of `groups`. A program takes and returns all parts, laid end to end along the dimension named above; an argument that names none is the same for every part. Nothing has to cross between parts.
Inputs may be any that keep to these rules, and one draw needn't show every extreme that they name: `gate_mask`: each entry says whether a block of 64 x 64 weights is kept (1) or zero (0); the share kept differs from block column to block column. `up_mask`: as gate_mask, drawn independently.
All inputs are finite; a program needn't handle non-finite values.
Results may differ from a plain program's by a relative error of at most 0.005.
Values may be sent and summed in bfloat16 or wider, within the bound.
A program may use at most 320 MiB of HBM per device.

v0:
```python
import jax
import jax.numpy as jnp
from jax import lax
from jax.sharding import PartitionSpec as P

BLOCK = 64


def expand_blocks(mask):
    rows, cols = mask.shape
    width = cols * BLOCK
    col_ids = lax.broadcasted_iota(jnp.int32, (cols, width), 1) // BLOCK
    own_ids = lax.broadcasted_iota(jnp.int32, (cols, width), 0)
    spread = (col_ids == own_ids).astype(jnp.bfloat16)
    wide_cols = jnp.dot(
        mask.astype(jnp.bfloat16), spread, preferred_element_type=jnp.float32
    ).astype(jnp.bfloat16)
    wide = jnp.broadcast_to(wide_cols[:, None, :], (rows, BLOCK, width))
    return wide.reshape(rows * BLOCK, width)


def shards(tokens, gate_weight, up_weight, gate_mask, up_mask, cotangent):
    gate_wide = expand_blocks(gate_mask)
    up_wide = expand_blocks(up_mask)
    gate_kept = gate_weight * gate_wide
    up_kept = up_weight * up_wide
    own_rows = lax.all_gather(tokens, "tensor", axis=1, tiled=True)
    half_block = lax.all_to_all(own_rows, "dp", split_axis=1, concat_axis=0, tiled=True)
    gate_full, up_full = (
        lax.all_gather(gate_kept, "dp", axis=0, tiled=True),
        lax.all_gather(up_kept, "dp", axis=0, tiled=True),
    )
    gate = jnp.dot(own_rows, gate_full, preferred_element_type=jnp.float32)
    up = jnp.dot(own_rows, up_full, preferred_element_type=jnp.float32)
    sig = jax.nn.sigmoid(gate)
    act = gate * sig
    hidden = (act * up).astype(jnp.bfloat16)
    grad_out = cotangent.astype(jnp.float32)
    d_gate = (grad_out * up * sig * (1.0 + gate * (1.0 - sig))).astype(jnp.bfloat16)
    d_up = (grad_out * act).astype(jnp.bfloat16)
    gate_all, up_all = (
        lax.all_gather(d_gate, "dp", axis=0, tiled=True),
        lax.all_gather(d_up, "dp", axis=0, tiled=True),
    )
    total = jnp.einsum("dh,th->dt", gate_full, d_gate, preferred_element_type=jnp.float32)
    input_terms = lax.psum_scatter(
        total + jnp.einsum("dh,th->dt", up_full, d_up, preferred_element_type=jnp.float32),
        "tensor",
        scatter_dimension=0,
        tiled=True,
    )
    grad_input = input_terms.T.astype(jnp.bfloat16)
    grad_gate = jnp.einsum("td,th->dh", half_block, gate_all, preferred_element_type=jnp.float32)
    grad_up = jnp.einsum("td,th->dh", half_block, up_all, preferred_element_type=jnp.float32)
    grad_gate = (grad_gate * gate_wide.astype(jnp.float32)).astype(jnp.bfloat16)
    grad_up = (grad_up * up_wide.astype(jnp.float32)).astype(jnp.bfloat16)
    return (hidden, grad_input, grad_gate, grad_up)


def solution(mesh):
    in_specs = (
        P(("groups", "dp"), "tensor"),
        P("dp", "tensor"),
        P("dp", "tensor"),
        P("dp", "tensor"),
        P("dp", "tensor"),
        P(("groups", "dp"), "tensor"),
    )
    out_specs = (
        P(("groups", "dp"), "tensor"),
        P(("groups", "dp"), "tensor"),
        P("dp", ("groups", "tensor")),
        P("dp", ("groups", "tensor")),
    )
    return jax.shard_map(shards, mesh=mesh, in_specs=in_specs, out_specs=out_specs, check_vma=False)
```

profile of v0, /device:TPU:8, one launch (start us, length us, event | category | flops | bytes accessed | tf_op | source)
XLA Modules:
  0.0 362.1 jit_solution(17467973323611626309)
XLA Ops:
  7.2 0.0 all-gather.8.cloned.1.call-start
  7.2 1.8 copy.26
  9.0 0.0 all-gather.8.cloned.1.call-update
  9.0 0.0 all-gather.6.cloned.1.call-start
  9.1 1.0 fusion.2
  10.1 13.9 %bitcast_multiply_fusion.3 = bf16[4096,2048]{1,0:T(8,128)(2,1)} fusion(bf16[4096,2048]{1,0:T(8,128)(2,1)} %param.7, bf16[64,2048]{1,0:T(8,128)(2,1)S(1)} %fusion.2), kind=kLoop, calls=%fused_computation.6 | loop fusion | flops 8388608 | bytes 33816576 | tf_op jit(solution)/shard_map/mul | solution.py:25
  24.0 0.0 copy-start.4
  24.0 0.0 all-gather.6.cloned.1.call-update
  24.0 0.0 all-gather.10.cloned.1.call-start
  24.1 0.6 copy-done.4
  24.7 0.3 fusion.3
  25.0 13.9 %bitcast_multiply_fusion.2 = bf16[4096,2048]{1,0:T(8,128)(2,1)} fusion(bf16[4096,2048]{1,0:T(8,128)(2,1)} %param.8, bf16[64,2048]{1,0:T(8,128)(2,1)S(1)} %fusion.3), kind=kLoop, calls=%fused_computation.5 | loop fusion | flops 8388608 | bytes 33816576 | tf_op jit(solution)/shard_map/mul | solution.py:26
  38.8 0.0 copy-start.3
  38.8 0.0 all-gather.10.cloned.1.call-update
  38.9 0.0 all-gather.12.cloned.1.call-start
  38.9 1.0 copy-done.3
  39.9 1.0 copy.27
  40.9 20.3 %all-gather.8.cloned.1.call-done = bf16[128,8192]{0,1:T(8,128)(2,1)} async-done(((bf16[128,1024]{0,1:T(8,128)(2,1)}), bf16[128,8192]{0,1:T(8,128)(2,1)}) %all-gather.8.cloned.1.call-update) | async-done | bytes 2097168 | tf_op jit(solution)/shard_map/all_gather | solution.py:27
  61.2 0.0 copy-start.1
  61.2 52.1 %all-gather.6.cloned.1.call-done = bf16[8192,2048]{1,0:T(8,128)(2,1)} async-done(((bf16[4096,2048]{1,0:T(8,128)(2,1)}), bf16[8192,2048]{1,0:T(8,128)(2,1)}) %all-gather.6.cloned.1.call-update) | async-done | bytes 33554448 | tf_op jit(solution)/shard_map/all_gather | solution.py:30
  113.3 18.2 %convolution_bitcast_fusion.1 = f32[128,2048]{0,1:T(8,128)} fusion(bf16[8192,2048]{1,0:T(8,128)(2,1)} %all-gather.6.cloned.1.call-done, bf16[128,8192]{0,1:T(8,128)(2,1)} %all-gather.8.cloned.1.call-done), kind=kOutput, calls=%fused_computation.8 | convolution fusion | flops 4294967296 | bytes 36700160 | tf_op jit(solution)/shard_map/dot_general | solution.py:33
  131.5 36.4 %all-gather.10.cloned.1.call-done = bf16[8192,2048]{1,0:T(8,128)(2,1)} async-done(((bf16[4096,2048]{1,0:T(8,128)(2,1)}), bf16[8192,2048]{1,0:T(8,128)(2,1)}) %all-gather.10.cloned.1.call-update) | async-done | bytes 33554448 | tf_op jit(solution)/shard_map/all_gather | solution.py:31
  167.9 0.0 copy-done.1
  167.9 17.0 %fusion.6 = (bf16[128,2048]{0,1:T(8,128)(2,1)}, bf16[128,2048]{0,1:T(8,128)(2,1)S(1)}, bf16[128,2048]{0,1:T(8,128)(2,1)}) fusion(bf16[128,2048]{0,1:T(8,128)(2,1)} %copy.27, f32[128,2048]{0,1:T(8,128)} %convolution_bitcast_fusion.1, bf16[8192,2048]{1,0:T(8,128)(2,1)} %all-gather.10.cloned.1.call-done, bf16[128,8192]{0,1:T(8,128)(2,1)S(1)} %copy-done.1), kind=kOutput, calls=%fused_computation.17 | convolution fusion | flops 4299161600 | bytes 38797312 | tf_op jit(solution)/shard_map/dot_general | solution.py:34
  184.9 0.0 all-gather.12.cloned.1.call-update
  185.0 0.0 all-gather.14.cloned.1.call-start
  185.0 0.5 all-gather.14.cloned.1.call-update
  185.5 0.0 copy-start
  185.6 0.2 reduce-scatter.2.cloned.1.call-start
  185.8 15.0 %fusion.20 = f32[8192,128]{1,0:T(8,128)S(1)} fusion(bf16[8192,2048]{1,0:T(8,128)(2,1)} %all-gather.6.cloned.1.call-done, bf16[128,2048]{0,1:T(8,128)(2,1)} %get-tuple-element.16), kind=kOutput, calls=%fused_computation.39 | convolution fusion | flops 4294967296 | bytes 38273024 | tf_op jit(solution)/shard_map/dh,th->dt/dot_general | solution.py:45
  200.8 0.0 copy-done
  200.8 18.1 %convolution_add_fusion = f32[8192,128]{1,0:T(8,128)} fusion(f32[8192,128]{1,0:T(8,128)S(1)} %fusion.20, bf16[8192,2048]{1,0:T(8,128)(2,1)} %all-gather.10.cloned.1.call-done, bf16[128,2048]{0,1:T(8,128)(2,1)S(1)} %copy-done), kind=kOutput, calls=%fused_computation.4 | convolution fusion | flops 4296015872 | bytes 42467328 | tf_op jit(solution)/shard_map/dh,th->dt/dot_general | solution.py:47
  218.9 0.0 reduce-scatter.2.cloned.1.call-update
  219.0 6.2 %broadcast_in_dim.4 = bf16[64,64,2048]{2,1,0:T(8,128)(2,1)} broadcast(bf16[64,2048]{1,0:T(8,128)(2,1)S(1)} %fusion.2), dimensions={0,2} | broadcast | bytes 17039360 | tf_op jit(solution)/shard_map/broadcast_in_dim | solution.py:18
  225.1 21.4 %copy.29 = bf16[4096,2048]{0,1:T(8,128)(2,1)} copy(bf16[4096,2048]{1,0:T(8,128)(2,1)} %bitcast.37) | data formatting | bytes 33554432 | tf_op jit(solution)/shard_map/reshape | solution.py:19
  246.5 6.1 %broadcast_in_dim.5 = bf16[64,64,2048]{2,1,0:T(8,128)(2,1)} broadcast(bf16[64,2048]{1,0:T(8,128)(2,1)S(1)} %fusion.3), dimensions={0,2} | broadcast | bytes 17039360 | tf_op jit(solution)/shard_map/broadcast_in_dim | solution.py:18
  252.6 0.0 copy-start.2
  252.6 21.3 %copy.30 = bf16[4096,2048]{0,1:T(8,128)(2,1)} copy(bf16[4096,2048]{1,0:T(8,128)(2,1)} %bitcast.38) | data formatting | bytes 33554432 | tf_op jit(solution)/shard_map/reshape | solution.py:19
  273.9 0.0 copy-done.2
  273.9 6.6 %all_to_all.19 = bf16[128,2,4096]{0,2,1:T(8,128)(2,1)} all-to-all(bf16[128,2,4096]{0,2,1:T(8,128)(2,1)S(1)} %bitcast.42), channel_id=1, replica_groups=mesh['groups'=2,'tensor'=8,'dp'=2] {'dp'}, dimensions={1} | all-to-all | bytes 4194304 | tf_op jit(solution)/shard_map/all_to_all | solution.py:28
  280.5 2.9 copy.28
  283.4 1.0 copy.31
  284.4 0.0 all-gather.12.cloned.1.call-done
  284.4 12.2 %fusion.1 = bf16[4096,2048]{0,1:T(8,128)(2,1)} fusion(bf16[4096,2048]{0,1:T(8,128)(2,1)} %copy.29, bf16[256,2048]{0,1:T(8,128)(2,1)} %all-gather.12.cloned.1.call-done, bf16[256,4096]{1,0:T(8,128)(2,1)S(1)} %bitcast.39), kind=kOutput, calls=%fused_computation.3 | convolution fusion | flops 4320133120 | bytes 36700160 | tf_op jit(solution)/shard_map/td,th->dh/dot_general | solution.py:53
  296.6 22.5 %copy.33 = bf16[4096,2048]{1,0:T(8,128)(2,1)} copy(bf16[4096,2048]{0,1:T(8,128)(2,1)} %fusion.1) | data formatting | bytes 33554432
  319.1 0.0 all-gather.14.cloned.1.call-done
  319.1 11.8 %fusion = bf16[4096,2048]{0,1:T(8,128)(2,1)} fusion(bf16[4096,2048]{0,1:T(8,128)(2,1)} %copy.30, bf16[256,2048]{0,1:T(8,128)(2,1)} %all-gather.14.cloned.1.call-done, bf16[256,4096]{1,0:T(8,128)(2,1)S(1)} %bitcast.40), kind=kOutput, calls=%fused_computation.1 | convolution fusion | flops 4320133120 | bytes 36700160 | tf_op jit(solution)/shard_map/td,th->dh/dot_general | solution.py:54
  330.9 22.4 %copy.34 = bf16[4096,2048]{1,0:T(8,128)(2,1)} copy(bf16[4096,2048]{0,1:T(8,128)(2,1)} %fusion) | data formatting | bytes 33554432
  353.3 0.0 reduce-scatter.2.cloned.1.call-done
  353.3 1.1 convert_bitcast_fusion
  354.4 0.9 copy.32
  (2 shorter events, 0.0 us)
Async XLA Ops:
  7.2 54.0 %all-gather.8.cloned.1.call-start = ((), (), s32[]{:S(2)}) async-start(), calls=%async_computation.3 | async-start | bytes 2359296 | tf_op jit(solution)/shard_map/all_gather | solution.py:27
  9.0 104.3 %all-gather.6.cloned.1.call-start = ((), (), s32[]{:S(2)}) async-start(), calls=%async_computation.2 | async-start | bytes 50331648 | tf_op jit(solution)/shard_map/all_gather | solution.py:30
  24.0 0.7 copy-start.4
  24.0 143.9 %all-gather.10.cloned.1.call-start = ((), (), s32[]{:S(2)}) async-start(), calls=%async_computation.4 | async-start | bytes 50331648 | tf_op jit(solution)/shard_map/all_gather | solution.py:31
  38.8 1.0 copy-start.3
  38.9 245.6 %all-gather.12.cloned.1.call-start = ((), (), s32[]{:S(2)}) async-start(), calls=%async_computation.6 | async-start | bytes 1572864 | tf_op jit(solution)/shard_map/all_gather | solution.py:42
  61.2 106.7 %copy-start.1 = (bf16[128,8192]{0,1:T(8,128)(2,1)S(1)}, bf16[128,8192]{0,1:T(8,128)(2,1)}, u32[]{:S(2)}) copy-start(bf16[128,8192]{0,1:T(8,128)(2,1)} %all-gather.8.cloned.1.call-done) | copy-start | bytes 6291460
  185.0 134.1 %all-gather.14.cloned.1.call-start = ((), (), s32[]{:S(2)}) async-start(), calls=%async_computation.7 | async-start | bytes 1572864 | tf_op jit(solution)/shard_map/all_gather | solution.py:43
  185.5 15.3 %copy-start = (bf16[128,2048]{0,1:T(8,128)(2,1)S(1)}, bf16[128,2048]{0,1:T(8,128)(2,1)}, u32[]{:S(2)}) copy-start(bf16[128,2048]{0,1:T(8,128)(2,1)} %get-tuple-element.18) | copy-start | bytes 1572868
  185.6 167.7 %reduce-scatter.2.cloned.1.call-start = ((), (), s32[]{:S(2)}) async-start(), calls=%async_computation.5 | async-start | bytes 4718592 | tf_op jit(solution)/shard_map/reduce_scatter | solution.py:46
  252.6 21.3 %copy-start.2 = (bf16[128,8192]{0,1:T(8,128)(2,1)S(1)}, bf16[128,8192]{0,1:T(8,128)(2,1)}, u32[]{:S(2)}) copy-start(bf16[128,8192]{0,1:T(8,128)(2,1)} %all-gather.8.cloned.1.call-done) | copy-start | bytes 6291460
Sparse Core Ops, SparseCore 0:
  10.7 50.4 all-gather.7
  63.3 49.9 all-gather.5
  115.5 52.3 all-gather.9
  185.1 10.1 all-gather.11
  196.7 10.1 all-gather.13
  219.1 89.0 reduce-scatter.1
where the time goes:
time: 366 us; the launch traced here: 362 us
  local copies, waits for them, and re-layouts  109 us (30%)
  waiting for transfers between devices  109 us (30%)
  matrix products  93.5 us (26%)
  other arithmetic  28.8 us (8%)
  between operations  14.2 us (4%)
  blocking collectives  6.58 us (2%)
    all_gather x1, waiting for transfers between devices, shards(): lax.all_gather(gate_kept, 'dp', axis=0, tiled=True)  52.1 us
    unnamed x16, local copies, waits for them, and re-layouts  51.2 us
    reshape x2, local copies, waits for them, and re-layouts, expand_blocks(): return wide.reshape(rows * BLOCK, width)  42.7 us
    all_gather x1, waiting for transfers between devices, shards(): lax.all_gather(up_kept, 'dp', axis=0, tiled=True)  36.4 us
    all_gather x1, waiting for transfers between devices, shards(): own_rows = lax.all_gather(tokens, 'tensor', axis=1, tiled=True)  20.3 us
    dot_general x1, matrix products, shards(): gate = jnp.dot(own_rows, gate_full, preferred_element_type=jnp.float32)  18.2 us
    dot_general x1, matrix products, shards(): jnp.einsum('dh,th->dt', up_full, d_up, preferred_element_type=jnp.float32)  18.1 us
    dot_general x1, matrix products, shards(): up = jnp.dot(own_rows, up_full, preferred_element_type=jnp.float32)  17 us
  transfers between devices with their start and end apart: 6, of which 3 were waited for; matrix products, arithmetic and copies ran while one was open for 58% of the time, Pallas kernels for 0%

commit v1 on v0

--- a/solution.py
+++ b/solution.py
@@ -1,6 +1,8 @@
 import jax
 import jax.numpy as jnp
 from jax import lax
+from jax.experimental import pallas as pl
+from jax.experimental.pallas import tpu as pltpu
 from jax.sharding import PartitionSpec as P
 
 BLOCK = 64
@@ -57,6 +59,466 @@
     return (hidden, grad_input, grad_gate, grad_up)
 
 
+MESH = pl.DeviceIdType.MESH
+TILE = 512
+
+
+def place():
+    t = lax.axis_index("tensor")
+    c = lax.axis_index("dp")
+    z = t // 2
+    x = t % 2
+    q = z + c * (3 - 2 * z)
+    step = 2 * (1 - 2 * c)
+    first = jnp.minimum(q, 1)
+    return t, c, x, q, {"tensor": t + 1 - 2 * x}, {"tensor": t + step}, {"tensor": t - step}, {"dp": 1 - c}, first
+
+
+def greet(q, xn, up, dn, sib):
+    barrier = pltpu.get_barrier_semaphore()
+    pl.semaphore_signal(barrier, inc=1, device_id=xn, device_id_type=MESH)
+    pl.semaphore_signal(barrier, inc=1, device_id=sib, device_id_type=MESH)
+
+    @pl.when(q < 3)
+    def _():
+        pl.semaphore_signal(barrier, inc=1, device_id=up, device_id_type=MESH)
+
+    @pl.when(q > 0)
+    def _():
+        pl.semaphore_signal(barrier, inc=1, device_id=dn, device_id_type=MESH)
+
+    ends = (q == 0) | (q == 3)
+
+    @pl.when(ends)
+    def _():
+        pl.semaphore_wait(barrier, 3)
+
+    @pl.when(jnp.logical_not(ends))
+    def _():
+        pl.semaphore_wait(barrier, 4)
+
+
+def remote(src, dst, send, recv, to):
+    return pltpu.make_async_remote_copy(
+        src_ref=src, dst_ref=dst, send_sem=send, recv_sem=recv, device_id=to, device_id_type=MESH
+    )
+
+
+def masked(w, m):
+    blocks, width = m.shape
+    wide = jnp.broadcast_to(m[:, None, :], (blocks, 16, width)).astype(jnp.bfloat16)
+    out = w.reshape(blocks, BLOCK // 16, 16, width) * wide[:, None]
+    return out.reshape(blocks * BLOCK, width)
+
+
+def forward_kernel(
+    tok_ref, wg_ref, wu_ref, mg_ref, mu_ref, cot_ref,
+    hid_ref, xt_ref, d_ref,
+    xbuf, wbuf, acc, rbuf, dbuf,
+    w_sem, sib_send, x_send, up_send, dn_send, own_recv, x_recv, a_send, a_recv, d_send, d_recv,
+):
+    t, c, x, q, xn, up, dn, sib, f = place()
+    s = 1 - f
+    kk = xbuf.shape[-1]
+    per = kk // BLOCK
+    tiles = acc.shape[0]
+
+    def slot(qs, o):
+        return ((qs + c * (1 - 2 * qs)) * 2 + (x + o * (1 - 2 * x)))
+
+    order = ((f, 0), (f, 1), (s, 0), (s, 1))
+
+    def weight_copy(i, gu):
+        qs, o = order[i]
+        src = (wg_ref, wu_ref)[gu]
+        rows = pl.ds(pl.multiple_of(slot(qs, o) * kk, kk), kk)
+        return pltpu.make_async_copy(src.at[rows, :], wbuf.at[gu, i], w_sem.at[gu, i])
+
+    for i in range(4):
+        for gu in range(2):
+            weight_copy(i, gu).start()
+
+    greet(q, xn, up, dn, sib)
+
+    @pl.when(q >= 2)
+    def _():
+        remote(tok_ref, xbuf.at[jnp.minimum(3 - q, 1), 0, 1], sib_send, own_recv.at[jnp.minimum(3 - q, 1), 1], sib).start()
+
+    @pl.when(q < 2)
+    def _():
+        xbuf[f, 0, 0] = tok_ref[...]
+
+    def x_copy(qs, h):
+        return remote(xbuf.at[qs, 0, h], xbuf.at[qs, 1, h], x_send.at[qs, h], x_recv.at[qs, h], xn)
+
+    def up_copy(qs, h):
+        return remote(xbuf.at[qs, 0, h], xbuf.at[qs, 0, h], up_send.at[qs, h], own_recv.at[qs, h], up)
+
+    def dn_copy(qs, h):
+        return remote(xbuf.at[qs, 0, h], xbuf.at[qs, 0, h], dn_send.at[h], own_recv.at[qs, h], dn)
+
+    def send_first(qs, h):
+        x_copy(qs, h).start()
+
+        @pl.when(q < 3)
+        def _():
+            up_copy(qs, h).start()
+
+        @pl.when(q == 1)
+        def _():
+            dn_copy(qs, h).start()
+
+    @pl.when(q >= 2)
+    def _():
+        up_copy(f, 0).wait_recv()
+
+    send_first(f, 0)
+    up_copy(f, 1).wait_recv()
+    send_first(f, 1)
+
+    def second(h):
+        up_copy(s, h).wait_recv()
+        x_copy(s, h).start()
+
+        @pl.when((q == 1) | (q == 2))
+        def _():
+            up_copy(s, h).start()
+
+    def block(i):
+        qs, o = order[i]
+        at = slot(qs, o)
+        if o == 1:
+            x_copy(qs, 0).wait_recv()
+            x_copy(qs, 1).wait_recv()
+        rows = pl.ds(pl.multiple_of(at * kk, kk), kk)
+        for h in range(2):
+            xt_ref[rows, pl.ds(h * xbuf.shape[3], xbuf.shape[3])] = xbuf[qs, o, h].T
+        weight_copy(i, 0).wait()
+        weight_copy(i, 1).wait()
+
+        def tile(j, _):
+            cols = pl.ds(pl.multiple_of(j * TILE, TILE), TILE)
+            xs = xbuf[qs, o].reshape(-1, kk)
+            for gu, m_ref in ((0, mg_ref), (1, mu_ref)):
+                m = m_ref[pl.ds(pl.multiple_of(at * per, per), per), cols]
+                w = masked(wbuf[gu, i, :, cols], m)
+                y = jnp.dot(xs, w, preferred_element_type=jnp.float32)
+                half = y.shape[0] // 2
+                if i == 0:
+                    acc[j, 0, gu] = y[:half]
+                    acc[j, 1, gu] = y[half:]
+                else:
+                    acc[j, 0, gu] += y[:half]
+                    acc[j, 1, gu] += y[half:]
+            if i == 3:
+                remote(acc.at[j, 1], rbuf.at[j], a_send.at[j], a_recv.at[j], sib).start()
+            return 0
+
+        lax.fori_loop(0, tiles, tile, 0)
+
+    block(0)
+    second(0)
+    second(1)
+    block(1)
+    block(2)
+    block(3)
+
+    def point(j, _):
+        cols = pl.ds(pl.multiple_of(j * TILE, TILE), TILE)
+        remote(acc.at[j, 1], rbuf.at[j], a_send.at[j], a_recv.at[j], sib).wait_recv()
+        gate = acc[j, 0, 0] + rbuf[j, 0]
+        upv = acc[j, 0, 1] + rbuf[j, 1]
+        sig = jax.nn.sigmoid(gate)
+        act = gate * sig
+        hid_ref[:, cols] = (act * upv).astype(jnp.bfloat16)
+        g = cot_ref[:, cols].astype(jnp.float32)
+        dg = (g * upv * sig * (1.0 + gate * (1.0 - sig))).astype(jnp.bfloat16)
+        du = (g * act).astype(jnp.bfloat16)
+        dbuf[j, 0, 0] = dg
+        dbuf[j, 0, 1] = du
+        remote(dbuf.at[j, 0], dbuf.at[j, 1], d_send.at[j], d_recv.at[j], sib).start()
+        d_ref[0, 0, :, cols] = dg
+        d_ref[1, 0, :, cols] = du
+        return 0
+
+    lax.fori_loop(0, tiles, point, 0)
+
+    def collect(j, _):
+        cols = pl.ds(pl.multiple_of(j * TILE, TILE), TILE)
+        remote(dbuf.at[j, 0], dbuf.at[j, 1], d_send.at[j], d_recv.at[j], sib).wait()
+        d_ref[0, 1, :, cols] = dbuf[j, 1, 0]
+        d_ref[1, 1, :, cols] = dbuf[j, 1, 1]
+        remote(acc.at[j, 1], rbuf.at[j], a_send.at[j], a_recv.at[j], sib).wait_send()
+        return 0
+
+    lax.fori_loop(0, tiles, collect, 0)
+
+    for h in range(2):
+        x_copy(f, h).wait_send()
+        x_copy(s, h).wait_send()
+
+        @pl.when(q < 3)
+        def _():
+            up_copy(f, h).wait_send()
+
+        @pl.when((q == 1) | (q == 2))
+        def _():
+            up_copy(s, h).wait_send()
+
+        @pl.when(q == 1)
+        def _():
+            dn_copy(f, h).wait_send()
+
+    @pl.when(q >= 2)
+    def _():
+        remote(tok_ref, xbuf.at[jnp.minimum(3 - q, 1), 0, 1], sib_send, own_recv.at[jnp.minimum(3 - q, 1), 1], sib).wait_send()
+
+
+def input_kernel(
+    d_ref, wg_ref, wu_ref, mg_ref, mu_ref,
+    out_ref,
+    wbuf, psum, xout, xin, zout, upin, dnin, fout, fin,
+    w_sem, x_send, x_recv, z_send, up_recv, dn_recv, f_send, f_recv,
+):
+    t, c, x, q, xn, up, dn, sib, f = place()
+    s = 1 - f
+    kk = psum.shape[-1]
+    per = kk // BLOCK
+
+    def slot(qs, o):
+        return ((qs + c * (1 - 2 * qs)) * 2 + (x + o * (1 - 2 * x)))
+
+    order = ((s, 1), (f, 1), (s, 0), (f, 0))
+
+    def weight_copy(i, gu):
+        qs, o = order[i]
+        src = (wg_ref, wu_ref)[gu]
+        rows = pl.ds(pl.multiple_of(slot(qs, o) * kk, kk), kk)
+        return pltpu.make_async_copy(src.at[rows, :], wbuf.at[gu, i], w_sem.at[gu, i])
+
+    for i in range(4):
+        for gu in range(2):
+            weight_copy(i, gu).start()
+
+    greet(q, xn, up, dn, sib)
+    part = 256
+    steps = kk // part
+
+    def block(i):
+        qs, o = order[i]
+        at = slot(qs, o)
+        weight_copy(i, 0).wait()
+        weight_copy(i, 1).wait()
+
+        def tile(j, _):
+            rows = pl.ds(pl.multiple_of(j * part, part), part)
+            total = None
+            for gu, m_ref in ((0, mg_ref), (1, mu_ref)):
+                wide = []
+                for b in range(part // BLOCK):
+                    m = m_ref[pl.ds(at * per + j * (part // BLOCK) + b, 1), :]
+                    mm = jnp.broadcast_to(m, (16, m.shape[1])).astype(jnp.bfloat16)
+                    w = wbuf[gu, i, pl.ds(pl.multiple_of(j * part + b * BLOCK, BLOCK), BLOCK), :]
+                    wide.append((w.reshape(BLOCK // 16, 16, -1) * mm[None]).reshape(BLOCK, -1))
+                w = jnp.concatenate(wide, axis=0)
+                y = lax.dot_general(
+                    d_ref[gu].reshape(-1, w.shape[1]), w, (((1,), (1,)), ((), ())),
+                    preferred_element_type=jnp.float32,
+                )
+                total = y if total is None else total + y
+            half = total.shape[0] // 2
+            for h in range(2):
+                value = total[h * half:(h + 1) * half]
+                if o == 1:
+                    xout[i, h, :, rows] = value.astype(jnp.bfloat16)
+                else:
+                    psum[i - 2, h, :, rows] = value
+            return 0
+
+        lax.fori_loop(0, steps, tile, 0)
+
+    def x_copy(k, h):
+        return remote(xout.at[k, h], xin.at[k, h], x_send.at[k, h], x_recv.at[k, h], xn)
+
+    def z_copy(k, h, to, dst, sem):
+        return remote(zout.at[k, h], dst, z_send.at[k, h], sem, to)
+
+    for k in range(2):
+        block(k)
+        for h in range(2):
+            x_copy(k, h).start()
+    block(2)
+    block(3)
+
+    for h in range(2):
+        x_copy(0, h).wait_recv()
+
+        @pl.when((q == 1) | (q == 2))
+        def _():
+            z_copy(0, h, dn, upin.at[s, h], up_recv.at[s, h]).wait_recv()
+            zout[0, h] = (psum[0, h] + xin[0, h].astype(jnp.float32) + upin[s, h].astype(jnp.float32)).astype(jnp.bfloat16)
+
+        @pl.when((q == 0) | (q == 3))
+        def _():
+            zout[0, h] = (psum[0, h] + xin[0, h].astype(jnp.float32)).astype(jnp.bfloat16)
+
+        @pl.when(q == 0)
+        def _():
+            z_copy(0, h, up, dnin.at[h], dn_recv.at[h]).start()
+
+        @pl.when(q > 0)
+        def _():
+            z_copy(0, h, dn, upin.at[s, h], up_recv.at[s, h]).start()
+
+    def final_copy():
+        return remote(fout, fin, f_send, f_recv, sib)
+
+    for h in (1, 0):
+        x_copy(1, h).wait_recv()
+        psum[1, h] += xin[1, h].astype(jnp.float32)
+
+        @pl.when(q < 3)
+        def _():
+            z_copy(1, h, dn, upin.at[f, h], up_recv.at[f, h]).wait_recv()
+            psum[1, h] += upin[f, h].astype(jnp.float32)
+
+        @pl.when(q == 1)
+        def _():
+            z_copy(0, h, up, dnin.at[h], dn_recv.at[h]).wait_recv()
+            psum[1, h] += dnin[h].astype(jnp.float32)
+
+        @pl.when(q >= 2)
+        def _():
+            zout[1, h] = psum[1, h].astype(jnp.bfloat16)
+            z_copy(1, h, dn, upin.at[f, h], up_recv.at[f, h]).start()
+
+        @pl.when(q < 2)
+        def _():
+            if h == 1:
+                fout[...] = psum[1, h].astype(jnp.bfloat16)
+                final_copy().start()
+            else:
+                out_ref[...] = psum[1, h].astype(jnp.bfloat16)
+
+    @pl.when(q >= 2)
+    def _():
+        final_copy().wait_recv()
+        out_ref[...] = fin[...]
+
+    @pl.when(q < 2)
+    def _():
+        final_copy().wait_send()
+
+    for h in range(2):
+        x_copy(0, h).wait_send()
+        x_copy(1, h).wait_send()
+        z_copy(0, h, dn, upin.at[s, h], up_recv.at[s, h]).wait_send()
+
+        @pl.when(q >= 2)
+        def _():
+            z_copy(1, h, dn, upin.at[f, h], up_recv.at[f, h]).wait_send()
+
+
+def weight_kernel(xt_ref, d_ref, mg_ref, mu_ref, gg_ref, gu_ref):
+    width = gg_ref.shape[1]
+    for j in range(width // TILE):
+        cols = pl.ds(j * TILE, TILE)
+        for gu, m_ref, o_ref in ((0, mg_ref, gg_ref), (1, mu_ref, gu_ref)):
+            y = jnp.dot(xt_ref[...], d_ref[gu, :, cols], preferred_element_type=jnp.float32)
+            o_ref[:, cols] = masked(y.astype(jnp.bfloat16), m_ref[:, cols])
+
+
+def spread_columns(mask):
+    cols = mask.shape[1]
+    width = cols * BLOCK
+    col_ids = lax.broadcasted_iota(jnp.int32, (cols, width), 1) // BLOCK
+    own_ids = lax.broadcasted_iota(jnp.int32, (cols, width), 0)
+    spread = (col_ids == own_ids).astype(jnp.bfloat16)
+    return jnp.dot(mask.astype(jnp.bfloat16), spread, preferred_element_type=jnp.float32)
+
+
+def kernel_shards(tokens, gate_weight, up_weight, gate_mask, up_mask, cotangent):
+    half, kk = tokens.shape
+    rows, width = gate_weight.shape
+    tiles = width // TILE
+    bf, f32 = jnp.bfloat16, jnp.float32
+    mg, mu = spread_columns(gate_mask), spread_columns(up_mask)
+    vmem = pl.BlockSpec(memory_space=pltpu.VMEM)
+    anyspec = pl.BlockSpec(memory_space=pl.ANY)
+    dma = pltpu.SemaphoreType.DMA
+    flops = 2 * 2 * 2 * half * rows * width
+    cost = pl.CostEstimate(flops=flops, bytes_accessed=4 * rows * width, transcendentals=half * width)
+    hidden, xt, d = pl.pallas_call(
+        forward_kernel,
+        out_shape=(
+            jax.ShapeDtypeStruct((half, width), bf),
+            jax.ShapeDtypeStruct((rows, 2 * half), bf),
+            jax.ShapeDtypeStruct((2, 2, half, width), bf),
+        ),
+        in_specs=[vmem, anyspec, anyspec, vmem, vmem, vmem],
+        out_specs=(vmem, vmem, vmem),
+        scratch_shapes=[
+            pltpu.VMEM((2, 2, 2, half, kk), bf),
+            pltpu.VMEM((2, 4, kk, width), bf),
+            pltpu.VMEM((tiles, 2, 2, half, TILE), f32),
+            pltpu.VMEM((tiles, 2, half, TILE), f32),
+            pltpu.VMEM((tiles, 2, 2, half, TILE), bf),
+            dma((2, 4)), dma, dma((2, 2)), dma((2, 2)), dma((2,)), dma((2, 2)), dma((2, 2)),
+            dma((tiles,)), dma((tiles,)), dma((tiles,)), dma((tiles,)),
+        ],
+        compiler_params=pltpu.CompilerParams(
+            collective_id=0, has_side_effects=True, vmem_limit_bytes=60 * 2**20
+        ),
+        cost_estimate=cost,
+    )(tokens, gate_weight, up_weight, mg, mu, cotangent)
+    block = (2, half, kk)
+    grad_input = pl.pallas_call(
+        input_kernel,
+        out_shape=jax.ShapeDtypeStruct((half, kk), bf),
+        in_specs=[vmem, anyspec, anyspec, vmem, vmem],
+        out_specs=vmem,
+        scratch_shapes=[
+            pltpu.VMEM((2, 4, kk, width), bf),
+            pltpu.VMEM((2,) + block, f32),
+            pltpu.VMEM((2,) + block, bf),
+            pltpu.VMEM((2,) + block, bf),
+            pltpu.VMEM((2,) + block, bf),
+            pltpu.VMEM((2,) + block, bf),
+            pltpu.VMEM(block, bf),
+            pltpu.VMEM((half, kk), bf),
+            pltpu.VMEM((half, kk), bf),
+            dma((2, 4)), dma((2, 2)), dma((2, 2)), dma((2, 2)), dma((2, 2)), dma((2,)), dma, dma,
+        ],
+        compiler_params=pltpu.CompilerParams(
+            collective_id=1, has_side_effects=True, vmem_limit_bytes=60 * 2**20
+        ),
+        cost_estimate=cost,
+    )(d, gate_weight, up_weight, mg, mu)
+    step = 512
+    d_all = d.reshape(2, 2 * half, width)
+    mask_spec = pl.BlockSpec((step // BLOCK, width), lambda i: (i, 0))
+    out_spec = pl.BlockSpec((step, width), lambda i: (i, 0))
+    grad_gate, grad_up = pl.pallas_call(
+        weight_kernel,
+        grid=(rows // step,),
+        out_shape=(jax.ShapeDtypeStruct((rows, width), bf),) * 2,
+        in_specs=[
+            pl.BlockSpec((step, 2 * half), lambda i: (i, 0)),
+            pl.BlockSpec((2, 2 * half, width), lambda i: (0, 0, 0)),
+            mask_spec,
+            mask_spec,
+        ],
+        out_specs=(out_spec, out_spec),
+        compiler_params=pltpu.CompilerParams(vmem_limit_bytes=48 * 2**20),
+        cost_estimate=cost,
+    )(xt, d_all, mg, mu)
+    return (hidden, grad_input, grad_gate, grad_up)
+
+
+def body(mesh):
+    return kernel_shards if mesh.shape["tensor"] == 8 and mesh.shape["dp"] == 2 else shards
+
+
 def solution(mesh):
     in_specs = (
         P(("groups", "dp"), "tensor"),
@@ -72,4 +534,4 @@
         P("dp", ("groups", "tensor")),
         P("dp", ("groups", "tensor")),
     )
-    return jax.shard_map(shards, mesh=mesh, in_specs=in_specs, out_specs=out_specs, check_vma=False)
+    return jax.shard_map(body(mesh), mesh=mesh, in_specs=in_specs, out_specs=out_specs, check_vma=False)

time: 366 us -> 110 us (0.30)
  waiting for transfers between devices: 109 us -> 0 us
  local copies, waits for them, and re-layouts: 109 us -> 5.65 us
  Pallas kernels: 0 us -> 99.7 us
  matrix products: 93.5 us -> 3.57 us
  other arithmetic: 28.8 us -> 0.01 us
  between operations: 14.2 us -> 0.69 us
  blocking collectives: 6.58 us -> 0 us
    all_gather x5 -> x0, waiting for transfers between devices: 109 us -> none  [the longest x1 52.1 us: shards(): lax.all_gather(gate_kept, 'dp', axis=0, tiled=True)]
    pallas_call x0 -> x3, Pallas kernels: none -> 99.7 us  [the longest x1 48.9 us: kernel_shards(): pl.pallas_call(input_kernel, out_shape=jax.ShapeDtypeStruct((half, kk), b...]
    dot_general x8 -> x2, matrix products: 93.5 us -> 3.57 us  [spread_columns(): jnp.dot(mask.astype(jnp.bfloat16), spread, preferred_element_type=jnp.flo...]
    unnamed x16 -> x12, local copies, waits for them, and re-layouts: 51.2 us -> 5.65 us
    reshape x2 -> x0, local copies, waits for them, and re-layouts: 42.7 us -> none  [expand_blocks(): return wide.reshape(rows * BLOCK, width)]
    mul x2 -> x0, other arithmetic: 27.8 us -> none  [the longest x1 13.9 us: shards(): gate_kept = gate_weight * gate_wide]
    broadcast_in_dim x2 -> x0, local copies, waits for them, and re-layouts: 12.3 us -> none  [expand_blocks(): wide = jnp.broadcast_to(wide_cols[:, None, :], (rows, BLOCK, width))]
    all_to_all x1 -> x0, blocking collectives: 6.58 us -> none  [shards(): lax.all_to_all(own_rows, 'dp', split_axis=1, concat_axis=0, tiled=True)]
  transfers between devices with their start and end apart: 6 -> 0, of which waited for: 3 -> 0; matrix products, arithmetic and copies ran while one was open for 58% -> 0% of each run, Pallas kernels for 0% -> 0%
where the time goes in v1:
time: 110 us
  Pallas kernels  99.7 us (91%)
  local copies, waits for them, and re-layouts  5.65 us (5%)
  matrix products  3.57 us (3%)
    pallas_call x1, Pallas kernels, kernel_shards(): pl.pallas_call(input_kernel, out_shape=jax.ShapeDtypeStruct((half, kk), b...  48.9 us
    pallas_call x1, Pallas kernels, kernel_shards(): pl.pallas_call(forward_kernel, out_shape=(jax.ShapeDtypeStruct((half, wid...  37.1 us
    pallas_call x1, Pallas kernels, kernel_shards(): pl.pallas_call(weight_kernel, grid=(rows // step,), out_shape=(jax.ShapeD...  13.7 us
    unnamed x12, local copies, waits for them, and re-layouts  5.65 us
    dot_general x2, matrix products, spread_columns(): jnp.dot(mask.astype(jnp.bfloat16), spread, preferred_element_type=jnp.flo...  3.57 us

profile of v1, /device:TPU:8, one launch (start us, length us, event | category | flops | bytes accessed | tf_op | source)
XLA Modules:
  0.0 109.6 jit_solution(18006438287987694615)
XLA Ops:
  0.7 1.8 %convolution_bitcast_fusion.mu_ref = f32[64,2048]{1,0:T(8,128)} fusion(s32[2048]{0:T(1024)S(1)} %get-tuple-element.14, s32[2048]{0:T(1024)S(1)} %get-tuple-element.15, pred[2048]{0:T(1024)(128)(4,1)S(1)} %fusion.10, s32[64,32]{0,1:T(8,128)} %param.10), kind=kOutput, calls=%fused_computation | convolution fusion | flops 8521728 | bytes 550912 | tf_op jit(solution)/shard_map/dot_general | solution.py:437
  2.4 1.8 %convolution_bitcast_fusion.1.mg_ref = f32[64,2048]{1,0:T(8,128)} fusion(s32[2048]{0:T(1024)S(1)} %get-tuple-element.14, s32[2048]{0:T(1024)S(1)} %get-tuple-element.15, pred[2048]{0:T(1024)(128)(4,1)S(1)} %fusion.10, s32[64,32]{0,1:T(8,128)} %param.9), kind=kOutput, calls=%fused_computation.1 | convolution fusion | flops 8521728 | bytes 550912 | tf_op jit(solution)/shard_map/dot_general | solution.py:437
  4.2 0.0 copy-start
  4.2 0.0 copy-start.1
  4.2 37.1 %shard_map.93 = (bf16[128,2048]{1,0:T(8,128)(2,1)}, bf16[4096,256]{1,0:T(8,128)(2,1)}, bf16[2,2,128,2048]{3,2,1,0:T(8,128)(2,1)}) custom-call(bf16[128,1024]{1,0:T(8,128)(2,1)} %tok_ref.1, bf16[4096,2048]{1,0:T(8,128)(2,1)} %wg_ref.3, bf16[4096,2048]{1,0:T(8,128)(2,1)} %wu_ref.3, f32[64,2048]{1,0:T(8,128)} %convolution_bitcast_fusion.1.mg_ref, ...), custom_call_target="tpu_custom_call" | custom-call | flops 8589934592 | bytes 33554432 | tf_op jit(solution)/shard_map/pallas_call | solution.py:451
  41.3 0.0 copy-done
  41.3 0.0 copy-done.1
  41.3 0.0 copy-start.2
  41.3 1.6 %copy-done.2 = bf16[2,2,128,2048]{3,2,1,0:T(8,128)(2,1)S(1)} copy-done((bf16[2,2,128,2048]{3,2,1,0:T(8,128)(2,1)S(1)}, bf16[2,2,128,2048]{3,2,1,0:T(8,128)(2,1)}, u32[]{:S(2)}) %copy-start.2) | copy-done | bytes 2097176
  42.9 0.0 copy-start.3
  42.9 1.6 %copy-done.3 = bf16[4096,256]{1,0:T(8,128)(2,1)S(1)} copy-done((bf16[4096,256]{1,0:T(8,128)(2,1)S(1)}, bf16[4096,256]{1,0:T(8,128)(2,1)}, u32[]{:S(2)}) %copy-start.3) | copy-done | bytes 2097176
  44.5 13.7 %shard_map.95 = (bf16[4096,2048]{1,0:T(8,128)(2,1)}, bf16[4096,2048]{1,0:T(8,128)(2,1)}) custom-call(bf16[4096,256]{1,0:T(8,128)(2,1)S(1)} %copy-done.3, bf16[2,256,2048]{2,1,0:T(8,128)(2,1)S(1)} %bitcast.5, f32[64,2048]{1,0:T(8,128)S(1)} %copy-done.1, f32[64,2048]{1,0:T(8,128)S(1)} %copy-done), custom_call_target="tpu_custom_call" | custom-call | flops 8589934592 | bytes 33554432 | tf_op jit(solution)/shard_map/pallas_call | solution.py:501
  58.2 0.0 copy-start.4
  58.2 48.9 %shard_map.94 = bf16[128,1024]{1,0:T(8,128)(2,1)} custom-call(bf16[2,2,128,2048]{3,2,1,0:T(8,128)(2,1)} %get-tuple-element.10.d_ref, bf16[4096,2048]{1,0:T(8,128)(2,1)} %wg_ref.3, bf16[4096,2048]{1,0:T(8,128)(2,1)} %wu_ref.3, f32[64,2048]{1,0:T(8,128)} %convolution_bitcast_fusion.1.mg_ref, f32[64,2048]{1,0:T(8,128)} %convolution_bitcast_fusion.mu_ref), custom_call_target="tpu_custom_call" | custom-call | flops 8589934592 | bytes 33554432 | tf_op jit(solution)/shard_map/pallas_call | solution.py:475
  107.1 0.0 copy-done.4
  107.1 0.8 copy.12
  107.9 1.7 %copy.13 = bf16[128,1024]{1,0:T(8,128)(2,1)} copy(bf16[128,1024]{1,0:T(8,128)(2,1)} %shard_map.94) | data formatting | bytes 524288
  (2 shorter events, 0.0 us)
Async XLA Ops:
  4.2 37.1 %copy-start = (f32[64,2048]{1,0:T(8,128)S(1)}, f32[64,2048]{1,0:T(8,128)}, u32[]{:S(2)}) copy-start(f32[64,2048]{1,0:T(8,128)} %convolution_bitcast_fusion.mu_ref) | copy-start | bytes 1572868
  4.2 37.1 %copy-start.1 = (f32[64,2048]{1,0:T(8,128)S(1)}, f32[64,2048]{1,0:T(8,128)}, u32[]{:S(2)}) copy-start(f32[64,2048]{1,0:T(8,128)} %convolution_bitcast_fusion.1.mg_ref) | copy-start | bytes 1572868
  41.3 1.6 %copy-start.2 = (bf16[2,2,128,2048]{3,2,1,0:T(8,128)(2,1)S(1)}, bf16[2,2,128,2048]{3,2,1,0:T(8,128)(2,1)}, u32[]{:S(2)}) copy-start(bf16[2,2,128,2048]{3,2,1,0:T(8,128)(2,1)} %get-tuple-element.10.d_ref) | copy-start | bytes 6291460
  42.9 1.6 %copy-start.3 = (bf16[4096,256]{1,0:T(8,128)(2,1)S(1)}, bf16[4096,256]{1,0:T(8,128)(2,1)}, u32[]{:S(2)}) copy-start(bf16[4096,256]{1,0:T(8,128)(2,1)} %get-tuple-element.11.xt_ref) | copy-start | bytes 6291460
  58.2 48.9 %copy-start.4 = (bf16[128,2048]{1,0:T(8,128)(2,1)S(1)}, bf16[128,2048]{1,0:T(8,128)(2,1)}, u32[]{:S(2)}) copy-start(bf16[128,2048]{1,0:T(8,128)(2,1)} %get-tuple-element.20) | copy-start | bytes 1572868

commit v2 on v1

--- a/solution.py
+++ b/solution.py
@@ -111,11 +111,12 @@
     return out.reshape(blocks * BLOCK, width)
 
 
-def forward_kernel(
+def main_kernel(
     tok_ref, wg_ref, wu_ref, mg_ref, mu_ref, cot_ref,
-    hid_ref, xt_ref, d_ref,
-    xbuf, wbuf, acc, rbuf, dbuf,
+    hid_ref, xt_ref, d_ref, out_ref,
+    xbuf, wbuf, mwide, acc, rbuf, dbuf, psum, xout, xin, zout, upin, dnin, fout, fin,
     w_sem, sib_send, x_send, up_send, dn_send, own_recv, x_recv, a_send, a_recv, d_send, d_recv,
+    r_send, r_recv, z_send, z_recv, n_recv, f_send, f_recv,
 ):
     t, c, x, q, xn, up, dn, sib, f = place()
     s = 1 - f
@@ -134,7 +135,7 @@
         rows = pl.ds(pl.multiple_of(slot(qs, o) * kk, kk), kk)
         return pltpu.make_async_copy(src.at[rows, :], wbuf.at[gu, i], w_sem.at[gu, i])
 
-    for i in range(4):
+    for i in range(2):
         for gu in range(2):
             weight_copy(i, gu).start()
 
@@ -175,6 +176,29 @@
     send_first(f, 0)
     up_copy(f, 1).wait_recv()
     send_first(f, 1)
+    for i in range(2, 4):
+        for gu in range(2):
+            weight_copy(i, gu).start()
+
+    mwide[0] = spread_columns(mg_ref[...])
+    mwide[1] = spread_columns(mu_ref[...])
+
+    def mask_block(i):
+        qs, o = order[i]
+        at = slot(qs, o)
+        weight_copy(i, 0).wait()
+        weight_copy(i, 1).wait()
+
+        def strip(b, _):
+            rows = pl.ds(pl.multiple_of(b * BLOCK, BLOCK), BLOCK)
+            for gu in range(2):
+                m = mwide[gu, pl.ds(at * per + b, 1), :]
+                wide = jnp.broadcast_to(m, (16, m.shape[1])).astype(jnp.bfloat16)
+                w = wbuf[gu, i, rows, :].reshape(BLOCK // 16, 16, m.shape[1])
+                wbuf[gu, i, rows, :] = (w * wide[None]).reshape(BLOCK, m.shape[1])
+            return 0
+
+        lax.fori_loop(0, per, strip, 0)
 
     def second(h):
         up_copy(s, h).wait_recv()
@@ -193,16 +217,12 @@
         rows = pl.ds(pl.multiple_of(at * kk, kk), kk)
         for h in range(2):
             xt_ref[rows, pl.ds(h * xbuf.shape[3], xbuf.shape[3])] = xbuf[qs, o, h].T
-        weight_copy(i, 0).wait()
-        weight_copy(i, 1).wait()
 
         def tile(j, _):
             cols = pl.ds(pl.multiple_of(j * TILE, TILE), TILE)
             xs = xbuf[qs, o].reshape(-1, kk)
-            for gu, m_ref in ((0, mg_ref), (1, mu_ref)):
-                m = m_ref[pl.ds(pl.multiple_of(at * per, per), per), cols]
-                w = masked(wbuf[gu, i, :, cols], m)
-                y = jnp.dot(xs, w, preferred_element_type=jnp.float32)
+            for gu in range(2):
+                y = jnp.dot(xs, wbuf[gu, i, :, cols], preferred_element_type=jnp.float32)
                 half = y.shape[0] // 2
                 if i == 0:
                     acc[j, 0, gu] = y[:half]
@@ -216,10 +236,14 @@
 
         lax.fori_loop(0, tiles, tile, 0)
 
+    mask_block(0)
+    second(0)
+    mask_block(1)
+    second(1)
     block(0)
-    second(0)
-    second(1)
+    mask_block(2)
     block(1)
+    mask_block(3)
     block(2)
     block(3)
 
@@ -253,179 +277,156 @@
 
     lax.fori_loop(0, tiles, collect, 0)
 
-    for h in range(2):
-        x_copy(f, h).wait_send()
-        x_copy(s, h).wait_send()
-
-        @pl.when(q < 3)
-        def _():
-            up_copy(f, h).wait_send()
-
-        @pl.when((q == 1) | (q == 2))
-        def _():
-            up_copy(s, h).wait_send()
-
-        @pl.when(q == 1)
-        def _():
-            dn_copy(f, h).wait_send()
-
-    @pl.when(q >= 2)
-    def _():
-        remote(tok_ref, xbuf.at[jnp.minimum(3 - q, 1), 0, 1], sib_send, own_recv.at[jnp.minimum(3 - q, 1), 1], sib).wait_send()
-
-
-def input_kernel(
-    d_ref, wg_ref, wu_ref, mg_ref, mu_ref,
-    out_ref,
-    wbuf, psum, xout, xin, zout, upin, dnin, fout, fin,
-    w_sem, x_send, x_recv, z_send, up_recv, dn_recv, f_send, f_recv,
-):
-    t, c, x, q, xn, up, dn, sib, f = place()
-    s = 1 - f
-    kk = psum.shape[-1]
-    per = kk // BLOCK
-
-    def slot(qs, o):
-        return ((qs + c * (1 - 2 * qs)) * 2 + (x + o * (1 - 2 * x)))
-
-    order = ((s, 1), (f, 1), (s, 0), (f, 0))
-
-    def weight_copy(i, gu):
-        qs, o = order[i]
-        src = (wg_ref, wu_ref)[gu]
-        rows = pl.ds(pl.multiple_of(slot(qs, o) * kk, kk), kk)
-        return pltpu.make_async_copy(src.at[rows, :], wbuf.at[gu, i], w_sem.at[gu, i])
-
-    for i in range(4):
-        for gu in range(2):
-            weight_copy(i, gu).start()
-
-    greet(q, xn, up, dn, sib)
-    part = 256
-    steps = kk // part
-
-    def block(i):
-        qs, o = order[i]
-        at = slot(qs, o)
-        weight_copy(i, 0).wait()
-        weight_copy(i, 1).wait()
-
+    steps, part = xout.shape[1], xout.shape[3]
+    half = xout.shape[2] // 2
+
+    def r_copy(k, j):
+        return remote(xout.at[k, j], xin.at[k, j], r_send.at[k, j], r_recv.at[k, j], xn)
+
+    def z_copy(k, j):
+        qs = (s, f)[k]
+        return remote(zout.at[k, j], upin.at[qs, j], z_send.at[k, j], z_recv.at[qs, j], dn)
+
+    def n_copy(j):
+        return remote(zout.at[0, j], dnin.at[j], z_send.at[0, j], n_recv.at[j], up)
+
+    def f_copy(j):
+        return remote(fout.at[j], fin.at[j], f_send.at[j], f_recv.at[j], sib)
+
+    def partial(i, k, away):
         def tile(j, _):
             rows = pl.ds(pl.multiple_of(j * part, part), part)
             total = None
-            for gu, m_ref in ((0, mg_ref), (1, mu_ref)):
-                wide = []
-                for b in range(part // BLOCK):
-                    m = m_ref[pl.ds(at * per + j * (part // BLOCK) + b, 1), :]
-                    mm = jnp.broadcast_to(m, (16, m.shape[1])).astype(jnp.bfloat16)
-                    w = wbuf[gu, i, pl.ds(pl.multiple_of(j * part + b * BLOCK, BLOCK), BLOCK), :]
-                    wide.append((w.reshape(BLOCK // 16, 16, -1) * mm[None]).reshape(BLOCK, -1))
-                w = jnp.concatenate(wide, axis=0)
+            for gu in range(2):
+                w = wbuf[gu, i, rows, :]
                 y = lax.dot_general(
                     d_ref[gu].reshape(-1, w.shape[1]), w, (((1,), (1,)), ((), ())),
                     preferred_element_type=jnp.float32,
                 )
                 total = y if total is None else total + y
-            half = total.shape[0] // 2
-            for h in range(2):
-                value = total[h * half:(h + 1) * half]
-                if o == 1:
-                    xout[i, h, :, rows] = value.astype(jnp.bfloat16)
-                else:
-                    psum[i - 2, h, :, rows] = value
+            if away:
+                xout[k, j] = total.astype(jnp.bfloat16)
+                r_copy(k, j).start()
+            else:
+                psum[k, j] = total
             return 0
 
         lax.fori_loop(0, steps, tile, 0)
 
-    def x_copy(k, h):
-        return remote(xout.at[k, h], xin.at[k, h], x_send.at[k, h], x_recv.at[k, h], xn)
-
-    def z_copy(k, h, to, dst, sem):
-        return remote(zout.at[k, h], dst, z_send.at[k, h], sem, to)
-
-    for k in range(2):
-        block(k)
-        for h in range(2):
-            x_copy(k, h).start()
-    block(2)
-    block(3)
+    partial(3, 0, True)
+    partial(1, 1, True)
+    partial(2, 0, False)
+    partial(0, 1, False)
+
+    def hop(j, _):
+        r_copy(0, j).wait_recv()
+        psum[0, j] += xin[0, j].astype(jnp.float32)
+
+        @pl.when((q == 1) | (q == 2))
+        def _():
+            z_copy(0, j).wait_recv()
+            psum[0, j] += upin[s, j].astype(jnp.float32)
+
+        zout[0, j] = psum[0, j].astype(jnp.bfloat16)
+
+        @pl.when(q == 0)
+        def _():
+            n_copy(j).start()
+
+        @pl.when(q > 0)
+        def _():
+            z_copy(0, j).start()
+
+        return 0
+
+    lax.fori_loop(0, steps, hop, 0)
+
+    def last(j, _):
+        r_copy(1, j).wait_recv()
+        psum[1, j] += xin[1, j].astype(jnp.float32)
+
+        @pl.when(q < 3)
+        def _():
+            z_copy(1, j).wait_recv()
+            psum[1, j] += upin[f, j].astype(jnp.float32)
+
+        @pl.when(q == 1)
+        def _():
+            n_copy(j).wait_recv()
+            psum[1, j] += dnin[j].astype(jnp.float32)
+
+        @pl.when(q >= 2)
+        def _():
+            zout[1, j] = psum[1, j].astype(jnp.bfloat16)
+            z_copy(1, j).start()
+
+        @pl.when(q < 2)
+        def _():
+            fout[j] = psum[1, j, half:].astype(jnp.bfloat16)
+            f_copy(j).start()
+            out_ref[:, pl.ds(pl.multiple_of(j * part, part), part)] = psum[1, j, :half].astype(jnp.bfloat16)
+
+        return 0
+
+    lax.fori_loop(0, steps, last, 0)
+
+    def finish(j, _):
+        @pl.when(q >= 2)
+        def _():
+            f_copy(j).wait_recv()
+            out_ref[:, pl.ds(pl.multiple_of(j * part, part), part)] = fin[j]
+            z_copy(1, j).wait_send()
+
+        @pl.when(q < 2)
+        def _():
+            f_copy(j).wait_send()
+
+        r_copy(0, j).wait_send()
+        r_copy(1, j).wait_send()
+        z_copy(0, j).wait_send()
+        return 0
+
+    lax.fori_loop(0, steps, finish, 0)
 
     for h in range(2):
-        x_copy(0, h).wait_recv()
+        x_copy(f, h).wait_send()
+        x_copy(s, h).wait_send()
+
+        @pl.when(q < 3)
+        def _():
+            up_copy(f, h).wait_send()
 
         @pl.when((q == 1) | (q == 2))
         def _():
-            z_copy(0, h, dn, upin.at[s, h], up_recv.at[s, h]).wait_recv()
-            zout[0, h] = (psum[0, h] + xin[0, h].astype(jnp.float32) + upin[s, h].astype(jnp.float32)).astype(jnp.bfloat16)
-
-        @pl.when((q == 0) | (q == 3))
-        def _():
-            zout[0, h] = (psum[0, h] + xin[0, h].astype(jnp.float32)).astype(jnp.bfloat16)
-
-        @pl.when(q == 0)
-        def _():
-            z_copy(0, h, up, dnin.at[h], dn_recv.at[h]).start()
-
-        @pl.when(q > 0)
-        def _():
-            z_copy(0, h, dn, upin.at[s, h], up_recv.at[s, h]).start()
-
-    def final_copy():
-        return remote(fout, fin, f_send, f_recv, sib)
-
-    for h in (1, 0):
-        x_copy(1, h).wait_recv()
-        psum[1, h] += xin[1, h].astype(jnp.float32)
-
-        @pl.when(q < 3)
-        def _():
-            z_copy(1, h, dn, upin.at[f, h], up_recv.at[f, h]).wait_recv()
-            psum[1, h] += upin[f, h].astype(jnp.float32)
+            up_copy(s, h).wait_send()
 
         @pl.when(q == 1)
         def _():
-            z_copy(0, h, up, dnin.at[h], dn_recv.at[h]).wait_recv()
-            psum[1, h] += dnin[h].astype(jnp.float32)
-
-        @pl.when(q >= 2)
-        def _():
-            zout[1, h] = psum[1, h].astype(jnp.bfloat16)
-            z_copy(1, h, dn, upin.at[f, h], up_recv.at[f, h]).start()
-
-        @pl.when(q < 2)
-        def _():
-            if h == 1:
-                fout[...] = psum[1, h].astype(jnp.bfloat16)
-                final_copy().start()
-            else:
-                out_ref[...] = psum[1, h].astype(jnp.bfloat16)
+            dn_copy(f, h).wait_send()
 
     @pl.when(q >= 2)
     def _():
-        final_copy().wait_recv()
-        out_ref[...] = fin[...]
-
-    @pl.when(q < 2)
-    def _():
-        final_copy().wait_send()
-
-    for h in range(2):
-        x_copy(0, h).wait_send()
-        x_copy(1, h).wait_send()
-        z_copy(0, h, dn, upin.at[s, h], up_recv.at[s, h]).wait_send()
-
-        @pl.when(q >= 2)
-        def _():
-            z_copy(1, h, dn, upin.at[f, h], up_recv.at[f, h]).wait_send()
-
-
-def weight_kernel(xt_ref, d_ref, mg_ref, mu_ref, gg_ref, gu_ref):
+        remote(tok_ref, xbuf.at[jnp.minimum(3 - q, 1), 0, 1], sib_send, own_recv.at[jnp.minimum(3 - q, 1), 1], sib).wait_send()
+
+
+def weight_kernel(xt_ref, d_ref, mg_ref, mu_ref, hid_ref, in_ref, gg_ref, gu_ref, hid_out, in_out, mwide):
+    i = pl.program_id(0)
+    per = xt_ref.shape[0] // BLOCK
+
+    @pl.when(i == 0)
+    def _():
+        mwide[0] = spread_columns(mg_ref[...])
+        mwide[1] = spread_columns(mu_ref[...])
+
+    hid_out[...] = hid_ref[...]
+    in_out[...] = in_ref[...]
     width = gg_ref.shape[1]
     for j in range(width // TILE):
         cols = pl.ds(j * TILE, TILE)
-        for gu, m_ref, o_ref in ((0, mg_ref, gg_ref), (1, mu_ref, gu_ref)):
+        for gu, o_ref in ((0, gg_ref), (1, gu_ref)):
             y = jnp.dot(xt_ref[...], d_ref[gu, :, cols], preferred_element_type=jnp.float32)
-            o_ref[:, cols] = masked(y.astype(jnp.bfloat16), m_ref[:, cols])
+            m = mwide[gu, pl.ds(pl.multiple_of(i * per, per), per), cols]
+            o_ref[:, cols] = masked(y.astype(jnp.bfloat16), m)
 
 
 def spread_columns(mask):
@@ -441,77 +442,79 @@
     half, kk = tokens.shape
     rows, width = gate_weight.shape
     tiles = width // TILE
+    part = 256
+    steps = kk // part
     bf, f32 = jnp.bfloat16, jnp.float32
-    mg, mu = spread_columns(gate_mask), spread_columns(up_mask)
     vmem = pl.BlockSpec(memory_space=pltpu.VMEM)
     anyspec = pl.BlockSpec(memory_space=pl.ANY)
     dma = pltpu.SemaphoreType.DMA
     flops = 2 * 2 * 2 * half * rows * width
-    cost = pl.CostEstimate(flops=flops, bytes_accessed=4 * rows * width, transcendentals=half * width)
-    hidden, xt, d = pl.pallas_call(
-        forward_kernel,
+    chunks = (steps, 2 * half, part)
+    hidden, xt, d, grad_input = pl.pallas_call(
+        main_kernel,
         out_shape=(
             jax.ShapeDtypeStruct((half, width), bf),
             jax.ShapeDtypeStruct((rows, 2 * half), bf),
             jax.ShapeDtypeStruct((2, 2, half, width), bf),
+            jax.ShapeDtypeStruct((half, kk), bf),
         ),
         in_specs=[vmem, anyspec, anyspec, vmem, vmem, vmem],
-        out_specs=(vmem, vmem, vmem),
+        out_specs=(vmem, vmem, vmem, vmem),
         scratch_shapes=[
             pltpu.VMEM((2, 2, 2, half, kk), bf),
             pltpu.VMEM((2, 4, kk, width), bf),
+            pltpu.VMEM((2, rows // BLOCK, width), f32),
             pltpu.VMEM((tiles, 2, 2, half, TILE), f32),
             pltpu.VMEM((tiles, 2, half, TILE), f32),
             pltpu.VMEM((tiles, 2, 2, half, TILE), bf),
+            pltpu.VMEM((2,) + chunks, f32),
+            pltpu.VMEM((2,) + chunks, bf),
+            pltpu.VMEM((2,) + chunks, bf),
+            pltpu.VMEM((2,) + chunks, bf),
+            pltpu.VMEM((2,) + chunks, bf),
+            pltpu.VMEM(chunks, bf),
+            pltpu.VMEM((steps, half, part), bf),
+            pltpu.VMEM((steps, half, part), bf),
             dma((2, 4)), dma, dma((2, 2)), dma((2, 2)), dma((2,)), dma((2, 2)), dma((2, 2)),
             dma((tiles,)), dma((tiles,)), dma((tiles,)), dma((tiles,)),
+            dma((2, steps)), dma((2, steps)), dma((2, steps)), dma((2, steps)),
+            dma((steps,)), dma((steps,)), dma((steps,)),
         ],
         compiler_params=pltpu.CompilerParams(
             collective_id=0, has_side_effects=True, vmem_limit_bytes=60 * 2**20
         ),
-        cost_estimate=cost,
-    )(tokens, gate_weight, up_weight, mg, mu, cotangent)
-    block = (2, half, kk)
-    grad_input = pl.pallas_call(
-        input_kernel,
-        out_shape=jax.ShapeDtypeStruct((half, kk), bf),
-        in_specs=[vmem, anyspec, anyspec, vmem, vmem],
-        out_specs=vmem,
-        scratch_shapes=[
-            pltpu.VMEM((2, 4, kk, width), bf),
-            pltpu.VMEM((2,) + block, f32),
-            pltpu.VMEM((2,) + block, bf),
-            pltpu.VMEM((2,) + block, bf),
-            pltpu.VMEM((2,) + block, bf),
-            pltpu.VMEM((2,) + block, bf),
-            pltpu.VMEM(block, bf),
-            pltpu.VMEM((half, kk), bf),
-            pltpu.VMEM((half, kk), bf),
-            dma((2, 4)), dma((2, 2)), dma((2, 2)), dma((2, 2)), dma((2, 2)), dma((2,)), dma, dma,
-        ],
-        compiler_params=pltpu.CompilerParams(
-            collective_id=1, has_side_effects=True, vmem_limit_bytes=60 * 2**20
+        cost_estimate=pl.CostEstimate(
+            flops=2 * flops, bytes_accessed=4 * rows * width, transcendentals=half * width
         ),
-        cost_estimate=cost,
-    )(d, gate_weight, up_weight, mg, mu)
+    )(tokens, gate_weight, up_weight, gate_mask, up_mask, cotangent)
     step = 512
-    d_all = d.reshape(2, 2 * half, width)
-    mask_spec = pl.BlockSpec((step // BLOCK, width), lambda i: (i, 0))
+    grid = rows // step
+    mask_spec = pl.BlockSpec(gate_mask.shape, lambda i: (0, 0))
     out_spec = pl.BlockSpec((step, width), lambda i: (i, 0))
-    grad_gate, grad_up = pl.pallas_call(
+    hid_spec = pl.BlockSpec((half // grid, width), lambda i: (i, 0))
+    in_spec = pl.BlockSpec((half // grid, kk), lambda i: (i, 0))
+    grad_gate, grad_up, hidden, grad_input = pl.pallas_call(
         weight_kernel,
-        grid=(rows // step,),
-        out_shape=(jax.ShapeDtypeStruct((rows, width), bf),) * 2,
+        grid=(grid,),
+        out_shape=(
+            jax.ShapeDtypeStruct((rows, width), bf),
+            jax.ShapeDtypeStruct((rows, width), bf),
+            jax.ShapeDtypeStruct((half, width), bf),
+            jax.ShapeDtypeStruct((half, kk), bf),
+        ),
         in_specs=[
             pl.BlockSpec((step, 2 * half), lambda i: (i, 0)),
             pl.BlockSpec((2, 2 * half, width), lambda i: (0, 0, 0)),
             mask_spec,
             mask_spec,
+            hid_spec,
+            in_spec,
         ],
-        out_specs=(out_spec, out_spec),
+        out_specs=(out_spec, out_spec, hid_spec, in_spec),
+        scratch_shapes=[pltpu.VMEM((2, rows // BLOCK, width), f32)],
         compiler_params=pltpu.CompilerParams(vmem_limit_bytes=48 * 2**20),
-        cost_estimate=cost,
-    )(xt, d_all, mg, mu)
+        cost_estimate=pl.CostEstimate(flops=flops, bytes_accessed=4 * rows * width, transcendentals=0),
+    )(xt, d.reshape(2, 2 * half, width), gate_mask, up_mask, hidden, grad_input)
     return (hidden, grad_input, grad_gate, grad_up)
 
 

time: 110 us -> 102 us (0.927)
  Pallas kernels: 99.7 us -> 92.1 us
  matrix products: 3.57 us -> 0 us
  local copies, waits for them, and re-layouts: 5.65 us -> 8 us
    pallas_call x3 -> x2, Pallas kernels: 99.7 us -> 92.1 us  [the longest x1 77.8 us: kernel_shards(): pl.pallas_call(main_kernel, out_shape=(jax.ShapeDtypeStruct((half, width)...]
    dot_general x2 -> x0, matrix products: 3.57 us -> none  [spread_columns(): jnp.dot(mask.astype(jnp.bfloat16), spread, preferred_element_type=jnp.flo...]
    unnamed x12 -> x14, local copies, waits for them, and re-layouts: 5.65 us -> 8 us
where the time goes in v2:
time: 102 us; the launch traced here: 101 us
  Pallas kernels  92.1 us (90%)
  local copies, waits for them, and re-layouts  8 us (8%)
    pallas_call x1, Pallas kernels, kernel_shards(): pl.pallas_call(main_kernel, out_shape=(jax.ShapeDtypeStruct((half, width)...  77.8 us
    pallas_call x1, Pallas kernels, kernel_shards(): pl.pallas_call(weight_kernel, grid=(grid,), out_shape=(jax.ShapeDtypeStru...  14.3 us
    unnamed x14, local copies, waits for them, and re-layouts  8 us

profile of v2, /device:TPU:8, one launch (start us, length us, event | category | flops | bytes accessed | tf_op | source)
XLA Modules:
  0.0 100.8 jit_solution(13432808675064166856)
XLA Ops:
  0.6 1.4 %copy.10.mg_ref = s32[64,32]{1,0:T(8,128)} copy(s32[64,32]{0,1:T(8,128)} %param.9) | data formatting | bytes 16384 | tf_op args[3]
  2.0 1.4 %copy.11.mu_ref = s32[64,32]{1,0:T(8,128)} copy(s32[64,32]{0,1:T(8,128)} %param.10) | data formatting | bytes 16384 | tf_op args[4]
  3.5 0.0 copy-start
  3.5 0.0 copy-start.1
  3.5 77.8 %shard_map.93 = (bf16[128,2048]{1,0:T(8,128)(2,1)}, bf16[4096,256]{1,0:T(8,128)(2,1)}, bf16[2,2,128,2048]{3,2,1,0:T(8,128)(2,1)}, bf16[128,1024]{1,0:T(8,128)(2,1)}) custom-call(bf16[128,1024]{1,0:T(8,128)(2,1)} %tok_ref.1, bf16[4096,2048]{1,0:T(8,128)(2,1)} %wg_ref.1, bf16[4096,2048]{1,0:T(8,128)(2,1)} %wu_ref.1, s32[64,32]{1,0:T(8,128)} %copy.10.mg_ref, ...), custom_call_target="tpu_custom_call" | custom-call | flops 17179869184 | bytes 33554432 | tf_op jit(solution)/shard_map/pallas_call | solution.py:453
  81.3 0.0 copy-done
  81.3 0.0 copy-done.1
  81.3 0.0 copy-start.2
  81.3 1.6 %copy-done.2 = bf16[2,2,128,2048]{3,2,1,0:T(8,128)(2,1)S(1)} copy-done((bf16[2,2,128,2048]{3,2,1,0:T(8,128)(2,1)S(1)}, bf16[2,2,128,2048]{3,2,1,0:T(8,128)(2,1)}, u32[]{:S(2)}) %copy-start.2) | copy-done | bytes 2097176
  82.9 0.0 copy-start.3
  82.9 1.6 %copy-done.3 = bf16[4096,256]{1,0:T(8,128)(2,1)S(1)} copy-done((bf16[4096,256]{1,0:T(8,128)(2,1)S(1)}, bf16[4096,256]{1,0:T(8,128)(2,1)}, u32[]{:S(2)}) %copy-start.3) | copy-done | bytes 2097176
  84.5 0.0 copy-start.4
  84.5 1.0 %copy-done.4 = bf16[128,2048]{1,0:T(8,128)(2,1)S(1)} copy-done((bf16[128,2048]{1,0:T(8,128)(2,1)S(1)}, bf16[128,2048]{1,0:T(8,128)(2,1)}, u32[]{:S(2)}) %copy-start.4) | copy-done | bytes 524312
  85.5 0.0 copy-start.5
  85.5 0.9 copy-done.5
  86.5 14.3 %shard_map.94 = (bf16[4096,2048]{1,0:T(8,128)(2,1)}, bf16[4096,2048]{1,0:T(8,128)(2,1)}, bf16[128,2048]{1,0:T(8,128)(2,1)}, bf16[128,1024]{1,0:T(8,128)(2,1)}) custom-call(bf16[4096,256]{1,0:T(8,128)(2,1)S(1)} %copy-done.3, bf16[2,256,2048]{2,1,0:T(8,128)(2,1)S(1)} %bitcast.1, s32[64,32]{1,0:T(8,128)S(1)} %copy-done, s32[64,32]{1,0:T(8,128)S(1)} %copy-done.1, ...), custom_call_target="tpu_custom_call" | custom-call | flops 8589934592 | bytes 33554432 | tf_op jit(solution)/shard_map/pallas_call | solution.py:496
Async XLA Ops:
  3.5 77.8 %copy-start = (s32[64,32]{1,0:T(8,128)S(1)}, s32[64,32]{1,0:T(8,128)}, u32[]{:S(2)}) copy-start(s32[64,32]{1,0:T(8,128)} %copy.10.mg_ref) | copy-start | bytes 24580
  3.5 77.8 %copy-start.1 = (s32[64,32]{1,0:T(8,128)S(1)}, s32[64,32]{1,0:T(8,128)}, u32[]{:S(2)}) copy-start(s32[64,32]{1,0:T(8,128)} %copy.11.mu_ref) | copy-start | bytes 24580
  81.3 1.6 %copy-start.2 = (bf16[2,2,128,2048]{3,2,1,0:T(8,128)(2,1)S(1)}, bf16[2,2,128,2048]{3,2,1,0:T(8,128)(2,1)}, u32[]{:S(2)}) copy-start(bf16[2,2,128,2048]{3,2,1,0:T(8,128)(2,1)} %get-tuple-element.13) | copy-start | bytes 6291460
  82.9 1.6 %copy-start.3 = (bf16[4096,256]{1,0:T(8,128)(2,1)S(1)}, bf16[4096,256]{1,0:T(8,128)(2,1)}, u32[]{:S(2)}) copy-start(bf16[4096,256]{1,0:T(8,128)(2,1)} %get-tuple-element.12.xt_ref) | copy-start | bytes 6291460
  84.5 1.0 %copy-start.4 = (bf16[128,2048]{1,0:T(8,128)(2,1)S(1)}, bf16[128,2048]{1,0:T(8,128)(2,1)}, u32[]{:S(2)}) copy-start(bf16[128,2048]{1,0:T(8,128)(2,1)} %get-tuple-element.14.hid_ref) | copy-start | bytes 1572868
  85.5 0.9 copy-start.5

commit v3 on v2

--- a/solution.py
+++ b/solution.py
@@ -512,7 +512,7 @@
         ],
         out_specs=(out_spec, out_spec, hid_spec, in_spec),
         scratch_shapes=[pltpu.VMEM((2, rows // BLOCK, width), f32)],
-        compiler_params=pltpu.CompilerParams(vmem_limit_bytes=48 * 2**20),
+        compiler_params=pltpu.CompilerParams(vmem_limit_bytes=63 * 2**20),
         cost_estimate=pl.CostEstimate(flops=flops, bytes_accessed=4 * rows * width, transcendentals=0),
     )(xt, d.reshape(2, 2 * half, width), gate_mask, up_mask, hidden, grad_input)
     return (hidden, grad_input, grad_gate, grad_up)

time: 102 us -> 98 us (0.961)
  local copies, waits for them, and re-layouts: 8 us -> 2.8 us
  Pallas kernels: 92.1 us -> 93.7 us
    unnamed x14 -> x2, local copies, waits for them, and re-layouts: 8 us -> 2.8 us
    pallas_call x1, Pallas kernels: 14.3 us -> 15.9 us  [kernel_shards(): pl.pallas_call(weight_kernel, grid=(grid,), out_shape=(jax.ShapeDtypeStru...]
where the time goes in v3:
time: 98 us; the launch traced here: 97.1 us
  Pallas kernels  93.7 us (96%)
  local copies, waits for them, and re-layouts  2.8 us (3%)
    pallas_call x1, Pallas kernels, kernel_shards(): pl.pallas_call(main_kernel, out_shape=(jax.ShapeDtypeStruct((half, width)...  77.8 us
    pallas_call x1, Pallas kernels, kernel_shards(): pl.pallas_call(weight_kernel, grid=(grid,), out_shape=(jax.ShapeDtypeStru...  15.9 us
    unnamed x2, local copies, waits for them, and re-layouts  2.8 us

profile of v3, /device:TPU:8, one launch (start us, length us, event | category | flops | bytes accessed | tf_op | source)
XLA Modules:
  0.0 97.1 jit_solution(11794780416074957477)
XLA Ops:
  0.6 1.4 %copy.10.mg_ref = s32[64,32]{1,0:T(8,128)} copy(s32[64,32]{0,1:T(8,128)} %param.9) | data formatting | bytes 16384 | tf_op args[3]
  2.0 1.4 %copy.11.mu_ref = s32[64,32]{1,0:T(8,128)} copy(s32[64,32]{0,1:T(8,128)} %param.10) | data formatting | bytes 16384 | tf_op args[4]
  3.4 77.8 %shard_map.93 = (bf16[128,2048]{1,0:T(8,128)(2,1)}, bf16[4096,256]{1,0:T(8,128)(2,1)}, bf16[2,2,128,2048]{3,2,1,0:T(8,128)(2,1)}, bf16[128,1024]{1,0:T(8,128)(2,1)}) custom-call(bf16[128,1024]{1,0:T(8,128)(2,1)} %tok_ref.1, bf16[4096,2048]{1,0:T(8,128)(2,1)} %wg_ref.1, bf16[4096,2048]{1,0:T(8,128)(2,1)} %wu_ref.1, s32[64,32]{1,0:T(8,128)} %copy.10.mg_ref, ...), custom_call_target="tpu_custom_call" | custom-call | flops 17179869184 | bytes 33554432 | tf_op jit(solution)/shard_map/pallas_call | solution.py:453
  81.2 15.9 %shard_map.94 = (bf16[4096,2048]{1,0:T(8,128)(2,1)}, bf16[4096,2048]{1,0:T(8,128)(2,1)}, bf16[128,2048]{1,0:T(8,128)(2,1)}, bf16[128,1024]{1,0:T(8,128)(2,1)}) custom-call(bf16[4096,256]{1,0:T(8,128)(2,1)} %get-tuple-element.12.xt_ref, bf16[2,256,2048]{2,1,0:T(8,128)(2,1)} %bitcast.1, s32[64,32]{1,0:T(8,128)} %copy.10.mg_ref, s32[64,32]{1,0:T(8,128)} %copy.11.mu_ref, ...), custom_call_target="tpu_custom_call" | custom-call | flops 8589934592 | bytes 33554432 | tf_op jit(solution)/shard_map/pallas_call | solution.py:496
